TPU v7x, 32 devices: a whole 2x2x4 slice. The times are simulated.
32 devices in a mesh: seq: 8 (over z, core), head: 4 (over y, x).
Axes of the slice: x: 2, y: 2, z: 4, core: 2. Of those that a mesh axis runs over, the one named last changes fastest.
Arguments:
- queries: bfloat16 [2048, 16384], P('seq', 'head'), may hold values from -8 to 8
- keys: bfloat16 [2048, 1024], P('seq'), may hold values from -8 to 8
- values: bfloat16 [2048, 1024], P('seq'), may hold values from -8 to 8
- query_map: bfloat16 [128, 128, 128], P('head'), may hold values from -3 to 3
- key_map: bfloat16 [8, 128, 128], replicated, may hold values from -3 to 3
- positions: int32 [2048], P('seq'), may hold values from 0 to 131071, as said below
Outputs:
- error_grad: bfloat16 [2048, 16384], P('seq', 'head')
Inputs may be any that keep to these rules, and one draw needn't show every extreme that they name: `positions`: each token's position is one more than the token before it, or 0 where a new document begins; the window begins inside a document that ends at position 131071, and at least one document begins inside the window.
All inputs are finite; a program needn't handle non-finite values.
Results may differ from a plain program's by a relative error of at most 0.0085.
Values may be sent and summed in bfloat16 or wider, within the bound.
A program may use at most 128 MiB of HBM per device.

v0:
```python
from functools import partial
import math

import jax
import jax.numpy as jnp
from jax import lax
from jax.sharding import PartitionSpec as P

QHEADS = 128
KVH = 8
LENGTH = 131072


epsilon = 1e-06
masked_score = -1e30
highest = lax.Precision.HIGHEST


def feature_map(inputs, weights, cosine_part, sine_part):
    projected = jnp.einsum("thd,hde->hte", inputs, weights, preferred_element_type=jnp.float32)
    mapped = jax.nn.elu(projected) + 1.0
    return jnp.concatenate([cosine_part * mapped, sine_part * mapped], axis=2).astype(jnp.bfloat16)


def keep_state(status):
    return status


def attend(status, query_block, query_place, key_block, value_block, key_place, scaling):
    running, weight_sum, weighted = status
    scores = (
        jnp.einsum("qgpd,kgd->gpqk", query_block, key_block, preferred_element_type=jnp.float32)
        * scaling
    )
    visible = query_place[:, None] >= key_place[None, :]
    scores = jnp.where(visible, scores, masked_score)
    largest = jnp.maximum(running, jnp.max(scores, axis=-1))
    weights = jnp.where(visible, jnp.exp(scores - largest[..., None]), 0.0)
    factor = jnp.exp(running - largest)
    weight_sum = weight_sum * factor + jnp.sum(weights, axis=-1)
    weighted = weighted * factor[..., None] + jnp.einsum(
        "gpqk,kgd->gpqd",
        weights.astype(jnp.bfloat16),
        value_block,
        preferred_element_type=jnp.float32,
    )
    return (largest, weight_sum, weighted)


def per_device(queries, keys, values, query_map, key_map, positions):
    tokens = queries.shape[0]
    head_dim = key_map.shape[1]
    local_heads = query_map.shape[0]
    group_size = QHEADS // KVH
    kv_local = max(1, local_heads // group_size)
    per_group = local_heads // kv_local
    device = lax.axis_index("seq")
    first_group = lax.axis_index("head") * local_heads // group_size
    keys_mine = lax.dynamic_slice_in_dim(keys, first_group * head_dim, kv_local * head_dim, 1)
    values_mine = lax.dynamic_slice_in_dim(values, first_group * head_dim, kv_local * head_dim, 1)
    width_query = queries.shape[1]
    teacher_queries, teacher_keys, teacher_values = (queries, keys_mine, values_mine)
    query_place = device * tokens + jnp.arange(tokens, dtype=jnp.int32)
    grouped = teacher_queries.reshape(tokens, kv_local, per_group, head_dim)
    scaling = 1.0 / math.sqrt(head_dim)
    start_state = (
        jnp.full((kv_local, per_group, tokens), masked_score, jnp.float32),
        jnp.zeros((kv_local, per_group, tokens), jnp.float32),
        jnp.zeros((kv_local, per_group, tokens, head_dim), jnp.float32),
    )
    running_state = start_state
    piece_keys = lax.all_gather(teacher_keys, "seq", axis=0, tiled=True)
    piece_values = lax.all_gather(teacher_values, "seq", axis=0, tiled=True)
    row_count = piece_keys.shape[0]
    block_keys = math.gcd(row_count, 1024)
    blocks = row_count // block_keys
    key_place = jnp.arange(row_count, dtype=jnp.int32).reshape(blocks, block_keys)
    key_blocks = piece_keys.reshape(blocks, block_keys, kv_local, head_dim)
    value_blocks = piece_values.reshape(blocks, block_keys, kv_local, head_dim)

    def advance(status, inputs):
        key_block, value_block, key_row = inputs
        beyond = jnp.min(key_row) > jnp.max(query_place)
        compute_block = partial(
            attend,
            query_block=grouped,
            query_place=query_place,
            key_block=key_block,
            value_block=value_block,
            key_place=key_row,
            scaling=scaling,
        )
        return (lax.cond(beyond, keep_state, compute_block, status), None)

    running_state, unused = lax.scan(advance, running_state, (key_blocks, value_blocks, key_place))
    running, weight_sum, weighted = running_state
    result = weighted / weight_sum[..., None]
    teacher_out = (
        jnp.transpose(result, (2, 0, 1, 3)).reshape(tokens, width_query).astype(jnp.bfloat16)
    )
    angles = 0.5 * math.pi / LENGTH * positions.astype(jnp.float32)
    cosine_part = jnp.cos(angles)[None, :, None]
    sine_part = jnp.sin(angles)[None, :, None]
    query_feats = feature_map(
        queries.reshape(tokens, local_heads, head_dim), query_map, cosine_part, sine_part
    )
    map_mine = lax.dynamic_slice_in_dim(key_map, first_group, kv_local, 0)
    values_grouped = values_mine.reshape(tokens, kv_local, head_dim)
    key_feats = feature_map(
        keys_mine.reshape(tokens, kv_local, head_dim), map_mine, cosine_part, sine_part
    )
    totals = jnp.einsum(
        "gtf,tgd->gfd", key_feats, values_grouped, preferred_element_type=jnp.float32
    )
    masses = jnp.sum(key_feats, axis=1, dtype=jnp.float32)
    total_piece = lax.all_gather(
        totals[None].astype(jnp.bfloat16), "seq", axis=0, tiled=True
    ).astype(jnp.float32)
    mass_piece = lax.all_gather(
        masses[None].astype(jnp.bfloat16), "seq", axis=0, tiled=True
    ).astype(jnp.float32)
    below = jnp.arange(total_piece.shape[0], dtype=jnp.int32) < device
    before = jnp.zeros_like(totals) + jnp.sum(
        jnp.where(below[:, None, None, None], total_piece, 0.0), axis=0
    )
    mass_before = jnp.zeros_like(masses) + jnp.sum(
        jnp.where(below[:, None, None], mass_piece, 0.0), axis=0
    )
    feats_grouped = query_feats.reshape(kv_local, per_group, tokens, 2 * head_dim)
    causal = jnp.arange(tokens)[:, None] >= jnp.arange(tokens)[None, :]
    inner_block = jnp.where(
        causal,
        jnp.einsum("gptf,gsf->gpts", feats_grouped, key_feats, preferred_element_type=jnp.float32),
        0.0,
    )
    feats_wide = feats_grouped.astype(jnp.float32)
    values_wide = values_grouped.astype(jnp.float32)
    numerator = jnp.einsum(
        "gpts,sgd->gptd", inner_block, values_wide, precision=highest
    ) + jnp.einsum("gptf,gfd->gptd", feats_wide, before, precision=highest)
    denominator = jnp.sum(inner_block, axis=-1) + jnp.einsum(
        "gptf,gf->gpt", feats_wide, mass_before, precision=highest
    )
    student = numerator / (denominator[..., None] + epsilon)
    student = jnp.transpose(student, (2, 0, 1, 3)).reshape(tokens, width_query)
    return (2.0 * (student - teacher_out.astype(jnp.float32))).astype(jnp.bfloat16)


def solution(mesh):
    in_specs = (
        P("seq", "head"),
        P("seq", None),
        P("seq", None),
        P("head", None, None),
        P(),
        P("seq"),
    )
    out_specs = P("seq", "head")
    return jax.shard_map(
        per_device, mesh=mesh, in_specs=in_specs, out_specs=out_specs, check_vma=False
    )
```

profile of v0, /device:TPU:31, one launch (start us, length us, event | category | flops | bytes accessed | tf_op | source)
XLA Modules:
  0.0 209.9 jit_solution(12819408450085885024)
XLA Ops:
  6.5 1.7 constant_dynamic-slice_fusion.1
  10.1 1.0 copy.47
  11.8 1.3 multiply_convert_fusion.3
  14.7 1.1 fusion.38
  16.5 8.1 %all-gather.2 = bf16[8,2,256]{2,1,0:T(2,128)(2,1)S(1)} all-gather(bf16[1,2,256]{2,1,0:T(2,128)(2,1)S(1)} %bitcast.97), channel_id=3, replica_groups=mesh['seq'=8,'head'=4] {'seq'}, dimensions={0}, use_global_device_ids=true | all-gather | bytes 9216 | tf_op jit(solution)/shard_map/all_gather | solution.py:119
  24.6 2.4 %copy.52 = bf16[256,4096]{0,1:T(8,128)(2,1)} copy(bf16[256,4096]{1,0:T(8,128)(2,1)S(1)} %copy-done.2) | data formatting | bytes 4194304 | tf_op args[0]
  27.0 3.0 %copy.54 = bf16[256,2,16,128]{3,0,2,1:T(8,128)(2,1)S(1)} copy(bf16[256,2,16,128]{0,3,2,1:T(8,128)(2,1)} %bitcast.88) | data formatting | bytes 4194304
  30.1 6.1 %multiply_convert_fusion.1 = (bf16[32,256,128]{1,2,0:T(8,128)(2,1)}, bf16[32,256,128]{1,2,0:T(8,128)(2,1)}) fusion(f32[256]{0:T(256)S(1)} %get-tuple-element.259, f32[256]{0:T(256)S(1)} %get-tuple-element.260, bf16[32,128,128]{2,1,0:T(8,128)(2,1)S(1)} %copy-done, bf16[256,4096]{1,0:T(8,128)(2,1)} %param.10), kind=kOutput, calls=%fused_computation.39 | convolution fusion | flops 276824064 | bytes 7342080 | tf_op jit(solution)/shard_map/thd,hde->hte/dot_general | solution.py:20
  36.2 3.9 %copy.41 = bf16[2,16,256,128]{3,2,1,0:T(8,128)(2,1)} copy(bf16[2,16,256,128]{2,3,1,0:T(8,128)(2,1)} %bitcast.91) | data formatting | bytes 4194304 | tf_op jit(solution)/shard_map/concatenate | solution.py:22
  40.1 4.0 %copy.42 = bf16[2,16,256,128]{3,2,1,0:T(8,128)(2,1)} copy(bf16[2,16,256,128]{2,3,1,0:T(8,128)(2,1)} %bitcast.90) | data formatting | bytes 4194304 | tf_op jit(solution)/shard_map/concatenate | solution.py:22
  44.2 5.8 %fusion.32 = f32[2,1,16,256]{3,1,2,0:T(1,128)S(1)} fusion(bf16[2,16,256,128]{3,2,1,0:T(8,128)(2,1)} %copy.42, bf16[2,16,256,128]{3,2,1,0:T(8,128)(2,1)} %copy.41, f32[2,256,1,1]{1,0,2,3:T(2,128)S(1)} %bitcast.98), kind=kOutput, calls=%fused_computation.46 | convolution fusion | flops 33554432 | bytes 4229120 | tf_op jit(solution)/shard_map/gptf,gf->gpt/dot_general | solution.py:141
  50.0 1.4 select_reduce_fusion
  52.0 5.8 %fusion.20 = f32[2,16,256,128]{2,3,1,0:T(8,128)} fusion(bf16[256,2,128,1]{0,2,3,1:T(8,128)(2,1)S(1)} %bitcast.94, f32[2,16,256,256]{2,3,1,0:T(8,128)S(1)} %get-tuple-element.262, pred[256,256]{0,1:T(8,128)(4,1)S(1)} %iota_compare_fusion), kind=kOutput, calls=%fused_computation.27 | convolution fusion | flops 3223322624 | bytes 12779520 | tf_op jit(solution)/shard_map/gpts,sgd->gptd/dot_general | solution.py:138
  57.8 1.3 reshape.73
  59.1 1.1 copy.55
  60.3 1.8 reshape.89
  62.1 2.1 %copy.53 = bf16[2,1024,2,128]{3,1,2,0:T(8,128)(2,1)} copy(bf16[2,1024,2,128]{1,0,3,2:T(2,128)(2,1)S(1)} %reshape.89) | data formatting | bytes 2097152
  64.2 14.3 %all-gather.11.cloned.1.call-done = bf16[16,256,128]{2,1,0:T(8,128)(2,1)} async-done(((bf16[2,256,128]{2,1,0:T(8,128)(2,1)}), bf16[16,256,128]{2,1,0:T(8,128)(2,1)}) %all-gather.11.cloned.1.call-update) | async-done | bytes 1048592 | tf_op jit(solution)/shard_map/all_gather | solution.py:116
  78.5 2.2 %fusion.31 = f32[2,256,128]{2,1,0:T(8,128)} fusion(bf16[8,2,256,128]{3,2,1,0:T(8,128)(2,1)} %bitcast.92, pred[8]{0:T(512)(128)(4,1)S(1)} %iota_compare_fusion.1), kind=kLoop, calls=%fused_computation.45 | loop fusion | flops 1507328 | bytes 1310728 | tf_op jit(solution)/shard_map/reduce_sum | solution.py:123
  80.8 2.5 %broadcast_in_dim.87 = f32[2,16,256,128]{3,2,1,0:T(8,128)} broadcast(f32[]{:T(128)} %constant.86.clone.1), dimensions={} | broadcast | bytes 4194308 | tf_op jit(solution)/shard_map/broadcast_in_dim | solution.py:69
  83.2 100.6 %while.16 = (s32[]{:T(128)}, f32[2,16,256]{2,1,0:T(8,128)S(1)}, f32[2,16,256]{2,1,0:T(8,128)S(1)}, f32[2,16,256,128]{3,2,1,0:T(8,128)}, s32[2,1024]{1,0:T(2,128)...) while((s32[]{:T(128)}, f32[2,16,256]{2,1,0:T(8,128)S(1)}, ...), condition=%wide.region_11.12_spmd.clone, body=%wide.region_5.11_spmd.clone.sunk | while | flops 4406395904 | bytes 113788168 | solution.py:95
  85.3 48.3 %conditional.3 = (f32[2,16,256]{2,1,0:T(8,128)S(1)}, f32[2,16,256]{2,1,0:T(8,128)S(1)}, f32[2,16,256,128]{3,2,1,0:T(8,128)}) conditional(s32[]{:T(128)} %convert_element_type.87, (s32[]{:T(128)}, s32[1,1024]{1,0:T(1,128)S(1)}, bf16[2,1024,2,128]{3,1,2,0:T(8,128)(2,1)}, s32[]{:T(128)}, bf16[256,2,16,128]{3,0,2,1:T(8,128)(2,1)S(1)}, ...), branch_computations={%region_7.9_spmd, %region_10.10_spmd} | conditional | flops 4406394880 | bytes 113713176 | solution.py:93
  85.5 14.3 %fusion.2 = (f32[2,16,256]{2,1,0:T(8,128)S(1)}, f32[2,1024,256,16]{2,1,3,0:T(8,128)}) fusion(pred[256,1024]{0,1:T(8,128)(4,1)S(1)} %broadcast_compare_fusion, bf16[256,2,16,128]{3,0,2,1:T(8,128)(2,1)S(1)} %get-tuple-element.158, bf16[2,1024,2,128]{3,1,2,0:T(8,128)(2,1)} %get-tuple-element.156, s32[]{:T(128)} %get-tuple-element.157), kind=kOutput, calls=%fused_computation.3 | convolution fusion | flops 2172641280 | bytes 36471296 | tf_op jit(solution)/shard_map/while/body/eval_jaxpr/cond/branch_0_fun/qgpd,kgd->gpqk/dot_general | solution.py:32
  99.9 15.0 %fusion.4 = f32[2,16,256]{2,1,0:T(8,128)S(1)} fusion(f32[2,1024,256,16]{2,1,3,0:T(8,128)} %get-tuple-element.254, f32[2,16,256]{2,1,0:T(8,128)S(1)} %max.4, pred[256,1024]{0,1:T(8,128)(4,1)S(1)} %broadcast_compare_fusion), kind=kLoop, calls=%fused_computation.5 | loop fusion | flops 41934848 | bytes 33882112 | tf_op jit(solution)/shard_map/while/body/eval_jaxpr/cond/branch_0_fun/reduce_sum | solution.py:40
  114.9 18.7 %multiply_add_fusion = f32[2,16,256,128]{3,2,1,0:T(8,128)} fusion(f32[2,16,256,128]{3,2,1,0:T(8,128)} %get-tuple-element.160, f32[2,1024,256,16]{2,1,3,0:T(8,128)} %get-tuple-element.254, f32[2,16,256]{2,1,0:T(8,128)S(1)} %max.4, pred[256,1024]{0,1:T(8,128)(4,1)S(1)} %broadcast_compare_fusion, f32[2,16,256]{2,1,0:T(8,128)S(1)} %get-tuple-element.250, ...), kind=kOutput, calls=%fused_computation.8 | convolution fusion | flops 2191523840 | bytes 42795520 | tf_op jit(solution)/shard_map/while/body/eval_jaxpr/cond/branch_0_fun/gpqk,kgd->gpqd/dot_general | solution.py:41
  135.6 48.2 %conditional.3 = (f32[2,16,256]{2,1,0:T(8,128)S(1)}, f32[2,16,256]{2,1,0:T(8,128)S(1)}, f32[2,16,256,128]{3,2,1,0:T(8,128)}) conditional(s32[]{:T(128)} %convert_element_type.87, (s32[]{:T(128)}, s32[1,1024]{1,0:T(1,128)S(1)}, bf16[2,1024,2,128]{3,1,2,0:T(8,128)(2,1)}, s32[]{:T(128)}, bf16[256,2,16,128]{3,0,2,1:T(8,128)(2,1)S(1)}, ...), branch_computations={%region_7.9_spmd, %region_10.10_spmd} | conditional | flops 4406394880 | bytes 113713176 | solution.py:93
  135.9 14.3 %fusion.2 = (f32[2,16,256]{2,1,0:T(8,128)S(1)}, f32[2,1024,256,16]{2,1,3,0:T(8,128)}) fusion(pred[256,1024]{0,1:T(8,128)(4,1)S(1)} %broadcast_compare_fusion, bf16[256,2,16,128]{3,0,2,1:T(8,128)(2,1)S(1)} %get-tuple-element.158, bf16[2,1024,2,128]{3,1,2,0:T(8,128)(2,1)} %get-tuple-element.156, s32[]{:T(128)} %get-tuple-element.157), kind=kOutput, calls=%fused_computation.3 | convolution fusion | flops 2172641280 | bytes 36471296 | tf_op jit(solution)/shard_map/while/body/eval_jaxpr/cond/branch_0_fun/qgpd,kgd->gpqk/dot_general | solution.py:32
  150.2 15.0 %fusion.4 = f32[2,16,256]{2,1,0:T(8,128)S(1)} fusion(f32[2,1024,256,16]{2,1,3,0:T(8,128)} %get-tuple-element.254, f32[2,16,256]{2,1,0:T(8,128)S(1)} %max.4, pred[256,1024]{0,1:T(8,128)(4,1)S(1)} %broadcast_compare_fusion), kind=kLoop, calls=%fused_computation.5 | loop fusion | flops 41934848 | bytes 33882112 | tf_op jit(solution)/shard_map/while/body/eval_jaxpr/cond/branch_0_fun/reduce_sum | solution.py:40
  165.2 18.6 %multiply_add_fusion = f32[2,16,256,128]{3,2,1,0:T(8,128)} fusion(f32[2,16,256,128]{3,2,1,0:T(8,128)} %get-tuple-element.160, f32[2,1024,256,16]{2,1,3,0:T(8,128)} %get-tuple-element.254, f32[2,16,256]{2,1,0:T(8,128)S(1)} %max.4, pred[256,1024]{0,1:T(8,128)(4,1)S(1)} %broadcast_compare_fusion, f32[2,16,256]{2,1,0:T(8,128)S(1)} %get-tuple-element.250, ...), kind=kOutput, calls=%fused_computation.8 | convolution fusion | flops 2191523840 | bytes 42795520 | tf_op jit(solution)/shard_map/while/body/eval_jaxpr/cond/branch_0_fun/gpqk,kgd->gpqd/dot_general | solution.py:41
  183.9 5.5 %copy.56 = f32[2,16,256,128]{2,3,1,0:T(8,128)} copy(f32[2,16,256,128]{3,2,1,0:T(8,128)} %get-tuple-element.178) | data formatting | bytes 8388608 | tf_op jit(solution)/shard_map/while | solution.py:95
  189.4 9.9 %fusion.25 = bf16[256,2,16,128]{0,3,2,1:T(8,128)(2,1)} fusion(f32[2,16,256,128]{2,3,1,0:T(8,128)} %fusion.20, f32[2,16,256,128]{2,3,1,0:T(8,128)} %copy.56, f32[2,16,256]{2,1,0:T(8,128)S(1)} %get-tuple-element.179, f32[256,2,16]{0,2,1:T(8,128)S(1)} %copy-done.9, bf16[2,16,256,128]{3,2,1,0:T(8,128)(2,1)} %copy.42, ...), kind=kOutput, calls=%fused_computation.34 | convolution fusion | flops 3238002688 | bytes 15007744 | tf_op jit(solution)/shard_map/gptf,gfd->gptd/dot_general | solution.py:140
  199.3 4.1 %copy.57 = bf16[256,4096]{1,0:T(8,128)(2,1)} copy(bf16[256,4096]{0,1:T(8,128)(2,1)} %bitcast.89) | data formatting | bytes 4194304 | tf_op jit(solution)/shard_map/mul | solution.py:146
  (54 shorter events, 7.5 us)
Async XLA Ops:
  6.5 23.6 %copy-start = (bf16[32,128,128]{2,1,0:T(8,128)(2,1)S(1)}, bf16[32,128,128]{2,1,0:T(8,128)(2,1)}, u32[]{:S(2)}) copy-start(bf16[32,128,128]{2,1,0:T(8,128)(2,1)} %param.13) | copy-start | bytes 3145732
  6.5 18.1 %copy-start.2 = (bf16[256,4096]{1,0:T(8,128)(2,1)S(1)}, bf16[256,4096]{1,0:T(8,128)(2,1)}, u32[]{:S(2)}) copy-start(bf16[256,4096]{1,0:T(8,128)(2,1)} %param.10) | copy-start | bytes 6291460
  6.5 51.3 %all-gather.9.cloned.1.call-start = ((), (), s32[]{:S(2)}) async-start(), calls=%async_computation.1 | async-start | bytes 1179648 | tf_op jit(solution)/shard_map/all_gather | solution.py:73
  8.3 52.0 %all-gather.7.cloned.1.call-start = ((), (), s32[]{:S(2)}) async-start(), calls=%async_computation | async-start | bytes 1179648 | tf_op jit(solution)/shard_map/all_gather | solution.py:72
  10.0 68.5 %all-gather.11.cloned.1.call-start = ((), (), s32[]{:S(2)}) async-start(), calls=%async_computation.2 | async-start | bytes 1179648 | tf_op jit(solution)/shard_map/all_gather | solution.py:116
  13.1 0.6 copy-start.7
  40.1 9.9 %copy-start.8 = (bf16[2,256,128]{1,2,0:T(8,128)(2,1)S(1)}, bf16[2,256,128]{1,2,0:T(8,128)(2,1)}, u32[]{:S(2)}) copy-start(bf16[2,256,128]{1,2,0:T(8,128)(2,1)} %copy-done.7) | copy-start | bytes 393220
  44.1 5.9 %copy-start.3 = (bf16[2,16,256,128]{3,2,1,0:T(8,128)(2,1)S(1)}, bf16[2,16,256,128]{3,2,1,0:T(8,128)(2,1)}, u32[]{:S(2)}) copy-start(bf16[2,16,256,128]{3,2,1,0:T(8,128)(2,1)} %copy.41) | copy-start | bytes 6291460
  44.1 5.9 %copy-start.5 = (bf16[2,16,256,128]{3,2,1,0:T(8,128)(2,1)S(1)}, bf16[2,16,256,128]{3,2,1,0:T(8,128)(2,1)}, u32[]{:S(2)}) copy-start(bf16[2,16,256,128]{3,2,1,0:T(8,128)(2,1)} %copy.42) | copy-start | bytes 6291460
  183.8 5.5 %copy-start.4 = (bf16[2,16,256,128]{3,2,1,0:T(8,128)(2,1)S(1)}, bf16[2,16,256,128]{3,2,1,0:T(8,128)(2,1)}, u32[]{:S(2)}) copy-start(bf16[2,16,256,128]{3,2,1,0:T(8,128)(2,1)} %copy.41) | copy-start | bytes 6291460
  183.8 5.5 %copy-start.6 = (f32[2,256,128]{2,1,0:T(8,128)S(1)}, f32[2,256,128]{2,1,0:T(8,128)}, u32[]{:S(2)}) copy-start(f32[2,256,128]{2,1,0:T(8,128)} %fusion.31) | copy-start | bytes 786436
  183.8 5.5 %copy-start.9 = (f32[256,2,16]{0,2,1:T(8,128)S(1)}, f32[256,2,16]{0,2,1:T(8,128)}, u32[]{:S(2)}) copy-start(f32[256,2,16]{0,2,1:T(8,128)} %fusion.42) | copy-start | bytes 98308
  189.4 14.0 %copy-start.1 = (bf16[32,128,128]{2,1,0:T(8,128)(2,1)S(1)}, bf16[32,128,128]{2,1,0:T(8,128)(2,1)}, u32[]{:S(2)}) copy-start(bf16[32,128,128]{2,1,0:T(8,128)(2,1)} %param.13) | copy-start | bytes 3145732
Sparse Core Ops, SparseCore 0:
  9.0 21.9 all-gather.8
  32.6 22.7 all-gather.6
  57.0 21.5 all-gather.10
where the time goes:
time: 212 us; the launch traced here: 210 us
  matrix products  97 us (46%)
  other arithmetic  37.4 us (18%)
  local copies, waits for them, and re-layouts  36.9 us (17%)
  waiting for transfers between devices  14.4 us (7%)
  between operations  13.3 us (6%)
  blocking collectives  8.14 us (4%)
  loops' own time  2.76 us (1%)
    dot_general x2, matrix products, attend(): jnp.einsum('gpqk,kgd->gpqd', weights.astype(jnp.bfloat16), value_block, p...  37.3 us
    reduce_sum x2, other arithmetic, attend(): weight_sum = weight_sum * factor + jnp.sum(weights, axis=-1)  30 us
    dot_general x2, matrix products, attend(): jnp.einsum('qgpd,kgd->gpqk', query_block, key_block, preferred_element_ty...  28.6 us
    all_gather x1, waiting for transfers between devices, per_device(): lax.all_gather(totals[None].astype(jnp.bfloat16), 'seq', axis=0, tiled=True)  14.3 us
    unnamed x25, local copies, waits for them, and re-layouts  10.1 us
    dot_general x1, matrix products, per_device(): jnp.einsum('gptf,gfd->gptd', feats_wide, before, precision=highest)  9.9 us
    all_gather x1, blocking collectives, per_device(): lax.all_gather(masses[None].astype(jnp.bfloat16), 'seq', axis=0, tiled=True)  8.14 us
    concatenate x2, local copies, waits for them, and re-layouts, feature_map(): jnp.concatenate([cosine_part * mapped, sine_part * mapped], axis=2)  7.93 us
  transfers between devices with their start and end apart: 3, of which 1 were waited for; matrix products, arithmetic and copies ran while one was open for 22% of the time, Pallas kernels for 0%

commit v1 on v0

v1 whole, which is shorter than its diff:
```python
import functools
import math

import jax
import jax.numpy as jnp
from jax import lax
from jax.experimental import pallas as pl
from jax.experimental.pallas import tpu as pltpu
from jax.sharding import PartitionSpec as P

QHEADS = 128
KVH = 8
LENGTH = 131072
epsilon = 1e-06
masked_score = -1e30
MESH = pl.DeviceIdType.MESH
LOG2E = 1.4426950408889634


def elu_plus_one(x):
    return jnp.where(x > 0.0, x + 1.0, jnp.exp2(jnp.minimum(x, 0.0) * LOG2E))


def angle_parts(positions):
    angles = (0.5 * math.pi / LENGTH) * positions.astype(jnp.float32)
    return jnp.cos(angles), jnp.sin(angles)


def nt_dot(a, b):
    return lax.dot_general(a, b, (((1,), (1,)), ((), ())), preferred_element_type=jnp.float32)


def nn_dot(a, b):
    return jnp.dot(a, b, preferred_element_type=jnp.float32)


def kernel(
    n, kv_local, per_group, unroll,
    q_ref, k_ref, v_ref, qmap_ref, kmap_ref, pos_ref, out_ref,
    kbuf, vbuf, pbuf, acc, top, cat, state, cosq, sinq,
    send_sem, recv_sem, fwd_sem,
):
    tokens = q_ref.shape[0]
    hd = qmap_ref.shape[1]
    heads = qmap_ref.shape[0]
    nz = n // 2
    me = lax.axis_index("seq")
    z = me // 2
    core = me % 2
    partner = z * 2 + 1 - core
    group0 = lax.axis_index("head") * heads // (QHEADS // KVH)
    width = kv_local * hd
    columns = pl.ds(pl.multiple_of(group0 * hd, hd), width)
    scaling = LOG2E / math.sqrt(hd)

    barrier = pltpu.get_barrier_semaphore()

    def greet(zp, carry):
        pl.semaphore_signal(barrier, inc=1, device_id={"seq": zp * 2 + core}, device_id_type=MESH)
        return carry

    lax.fori_loop(0, z, greet, 0)
    lax.fori_loop(z + 1, nz, greet, 0)
    pl.semaphore_signal(barrier, inc=1, device_id={"seq": partner}, device_id_type=MESH)
    pl.semaphore_wait(barrier, nz)

    own = (k_ref.at[:, columns], v_ref.at[:, columns], pos_ref)
    buffers = (kbuf, vbuf, pbuf)

    def own_copy(part, slot, target):
        return pltpu.make_async_remote_copy(
            src_ref=own[part], dst_ref=buffers[part].at[me],
            send_sem=send_sem.at[part, slot], recv_sem=recv_sem.at[part, me],
            device_id={"seq": target}, device_id_type=MESH,
        )

    def forward_copy(part, zp):
        block = zp * 2 + core
        return pltpu.make_async_remote_copy(
            src_ref=buffers[part].at[block], dst_ref=buffers[part].at[block],
            send_sem=fwd_sem.at[part, zp], recv_sem=recv_sem.at[part, block],
            device_id={"seq": partner}, device_id_type=MESH,
        )

    def arrival(part, block):
        return pltpu.make_async_remote_copy(
            src_ref=buffers[part].at[block], dst_ref=buffers[part].at[block],
            send_sem=send_sem.at[part, 0], recv_sem=recv_sem.at[part, block],
            device_id={"seq": partner}, device_id_type=MESH,
        )

    @pl.when(core == 0)
    def _():
        for part in range(3):
            own_copy(part, z, partner).start()

    def send_up(zp, carry):
        for part in range(3):
            own_copy(part, zp, zp * 2 + core).start()
        return carry

    lax.fori_loop(z + 1, nz, send_up, 0)

    ones = jnp.ones((tokens, hd), jnp.bfloat16)

    def key_feats(keys, group, positions):
        cosine, sine = angle_parts(positions)
        projected = nn_dot(keys, kmap_ref[group0 + group]).T
        mapped = elu_plus_one(projected)
        return jnp.concatenate([cosine * mapped, sine * mapped], axis=0).astype(jnp.bfloat16)

    tall = jnp.broadcast_to(pos_ref[...].astype(jnp.float32), (hd, tokens)).T
    cosine, sine = angle_parts(tall)
    cosq[...] = cosine
    sinq[...] = sine
    for g in range(kv_local):
        own_cols = pl.ds(pl.multiple_of((group0 + g) * hd, hd), hd)
        keys = k_ref[:, own_cols]
        values = jnp.concatenate([v_ref[:, own_cols], ones], axis=1)
        feats = key_feats(keys, g, pos_ref[...])
        state[g] = jnp.zeros((2 * hd, 2 * hd), jnp.float32)

        def own_body(i, carry, g=g, keys=keys, values=values, feats=feats):
            row = lax.broadcasted_iota(jnp.int32, (tokens, tokens), 0)
            col = lax.broadcasted_iota(jnp.int32, (tokens, tokens), 1)
            causal = row >= col
            for u in range(unroll):
                h = g * per_group + i * unroll + u
                q = q_ref[:, pl.ds(pl.multiple_of(h * hd, hd), hd)]
                scores = jnp.where(causal, nt_dot(q, keys) * scaling, masked_score)
                largest = jnp.max(scores, axis=1, keepdims=True)
                weights = jnp.exp2(scores - largest).astype(jnp.bfloat16)
                acc[h] = nn_dot(weights, values)
                top[h] = jnp.broadcast_to(largest, (tokens, hd))
                mapped = elu_plus_one(nn_dot(q, qmap_ref[h]))
                qf = jnp.concatenate([cosq[...] * mapped, sinq[...] * mapped], axis=1).astype(jnp.bfloat16)
                inner = jnp.where(causal, nn_dot(qf, feats), 0.0).astype(jnp.bfloat16)
                cat[h, :, :tokens] = inner
                cat[h, :, tokens:] = qf
            return carry

        lax.fori_loop(0, per_group // unroll, own_body, 0)

    def use_block(block):
        for g in range(kv_local):
            group_cols = slice(g * hd, (g + 1) * hd)
            keys = kbuf[block, :, group_cols]
            values = jnp.concatenate([vbuf[block, :, group_cols], ones], axis=1)
            feats = key_feats(keys, g, pbuf[block])
            state[g] += nn_dot(feats, values)

            def body(i, carry, g=g, keys=keys, values=values):
                for u in range(unroll):
                    h = g * per_group + i * unroll + u
                    q = q_ref[:, pl.ds(pl.multiple_of(h * hd, hd), hd)]
                    scores = nt_dot(q, keys) * scaling
                    before = top[h]
                    largest = jnp.maximum(before, jnp.max(scores, axis=1, keepdims=True))
                    factor = jnp.exp2(before - largest)
                    wide = jnp.concatenate([largest] * (tokens // hd), axis=1)
                    weights = jnp.exp2(scores - wide).astype(jnp.bfloat16)
                    acc[h] = acc[h] * jnp.concatenate([factor, factor], axis=1) + nn_dot(weights, values)
                    top[h] = largest
                return carry

            lax.fori_loop(0, per_group // unroll, body, 0)

    @pl.when(core == 1)
    def _():
        for part in range(3):
            arrival(part, partner).wait_recv()
        use_block(partner)

    def step(i, carry):
        zp = z - 1 - i // 2
        first = i % 2 == 0
        block = zp * 2 + jnp.where(first, core, 1 - core)
        for part in range(3):
            arrival(part, block).wait_recv()

        @pl.when(first)
        def _():
            for part in range(3):
                forward_copy(part, zp).start()

        use_block(block)
        return carry

    lax.fori_loop(0, 2 * z, step, 0)

    for g in range(kv_local):
        own_cols = pl.ds(pl.multiple_of((group0 + g) * hd, hd), hd)
        stacked = jnp.concatenate(
            [jnp.concatenate([v_ref[:, own_cols], ones], axis=1), state[g].astype(jnp.bfloat16)], axis=0
        )

        def last_body(i, carry, g=g, stacked=stacked):
            for u in range(unroll):
                h = g * per_group + i * unroll + u
                both = nn_dot(cat[h], stacked)
                student = both[:, :hd] / (both[:, hd:] + epsilon)
                teacher = (acc[h, :, :hd] / acc[h, :, hd:]).astype(jnp.bfloat16).astype(jnp.float32)
                out_ref[:, pl.ds(pl.multiple_of(h * hd, hd), hd)] = (2.0 * (student - teacher)).astype(jnp.bfloat16)
            return carry

        lax.fori_loop(0, per_group // unroll, last_body, 0)

    @pl.when(core == 0)
    def _():
        for part in range(3):
            own_copy(part, z, partner).wait_send()

    def sent(zp, carry):
        for part in range(3):
            own_copy(part, zp, zp * 2 + core).wait_send()
        return carry

    lax.fori_loop(z + 1, nz, sent, 0)

    def forwarded(zp, carry):
        for part in range(3):
            forward_copy(part, zp).wait_send()
        return carry

    lax.fori_loop(0, z, forwarded, 0)


def per_device(n, queries, keys, values, query_map, key_map, positions):
    tokens = queries.shape[0]
    hd = key_map.shape[1]
    heads = query_map.shape[0]
    kv_local = max(1, heads // (QHEADS // KVH))
    per_group = heads // kv_local
    unroll = math.gcd(per_group, 4)
    width = kv_local * hd
    vmem = pl.BlockSpec(memory_space=pltpu.VMEM)
    return pl.pallas_call(
        functools.partial(kernel, n, kv_local, per_group, unroll),
        out_shape=jax.ShapeDtypeStruct(queries.shape, jnp.bfloat16),
        in_specs=[vmem] * 6,
        out_specs=vmem,
        scratch_shapes=[
            pltpu.VMEM((n, tokens, width), jnp.bfloat16),
            pltpu.VMEM((n, tokens, width), jnp.bfloat16),
            pltpu.VMEM((n, 1, tokens), jnp.int32),
            pltpu.VMEM((heads, tokens, 2 * hd), jnp.float32),
            pltpu.VMEM((heads, tokens, hd), jnp.float32),
            pltpu.VMEM((heads, tokens, tokens + 2 * hd), jnp.bfloat16),
            pltpu.VMEM((kv_local, 2 * hd, 2 * hd), jnp.float32),
            pltpu.VMEM((tokens, hd), jnp.float32),
            pltpu.VMEM((tokens, hd), jnp.float32),
            pltpu.SemaphoreType.DMA((3, n)),
            pltpu.SemaphoreType.DMA((3, n)),
            pltpu.SemaphoreType.DMA((3, n)),
        ],
        compiler_params=pltpu.CompilerParams(
            collective_id=0, has_side_effects=True, vmem_limit_bytes=56 * 1024 * 1024
        ),
    )(queries, keys, values, query_map, key_map, positions.reshape(1, tokens))


def solution(mesh):
    in_specs = (
        P("seq", "head"),
        P("seq", None),
        P("seq", None),
        P("head", None, None),
        P(),
        P("seq"),
    )
    return jax.shard_map(
        functools.partial(per_device, mesh.shape["seq"]),
        mesh=mesh, in_specs=in_specs, out_specs=P("seq", "head"), check_vma=False,
    )
```

time: 212 us -> 66.3 us (0.31)
  matrix products: 97 us -> 0 us
  Pallas kernels: 0 us -> 63 us
  other arithmetic: 37.4 us -> 0 us
  local copies, waits for them, and re-layouts: 36.9 us -> 3.13 us
  waiting for transfers between devices: 14.4 us -> 0 us
  between operations: 13.3 us -> 0.01 us
  blocking collectives: 8.14 us -> 0 us
  loops' own time: 2.76 us -> 0 us
    dot_general x11 -> x0, matrix products: 97 us -> none  [the longest x2 37.3 us: attend(): jnp.einsum('gpqk,kgd->gpqd', weights.astype(jnp.bfloat16), value_block, p...]
    pallas_call x0 -> x1, Pallas kernels: none -> 63 us  [per_device(): pl.pallas_call(functools.partial(kernel, n, kv_local, per_group, unroll),...]
    reduce_sum x5 -> x0, other arithmetic: 33.4 us -> none  [the longest x2 30 us: attend(): weight_sum = weight_sum * factor + jnp.sum(weights, axis=-1)]
    all_gather x3 -> x0, waiting for transfers between devices: 14.3 us -> none  [the longest x1 14.3 us: per_device(): lax.all_gather(totals[None].astype(jnp.bfloat16), 'seq', axis=0, tiled=True)]
    all_gather x1 -> x0, blocking collectives: 8.14 us -> none  [per_device(): lax.all_gather(masses[None].astype(jnp.bfloat16), 'seq', axis=0, tiled=True)]
    concatenate x2 -> x0, local copies, waits for them, and re-layouts: 7.93 us -> none  [feature_map(): jnp.concatenate([cosine_part * mapped, sine_part * mapped], axis=2)]
    unnamed x25 -> x1, local copies, waits for them, and re-layouts: 10.1 us -> 3.13 us
    while x3 -> x0, local copies, waits for them, and re-layouts: 5.53 us -> none  [the longest x1 5.52 us: per_device(): lax.scan(advance, running_state, (key_blocks, value_blocks, key_place))]
  transfers between devices with their start and end apart: 3 -> 0, of which waited for: 1 -> 0; matrix products, arithmetic and copies ran while one was open for 22% -> 0% of each run, Pallas kernels for 0% -> 0%
where the time goes in v1:
time: 66.3 us; the launch traced here: 66.2 us
  Pallas kernels  63 us (95%)
  local copies, waits for them, and re-layouts  3.13 us (5%)
    pallas_call x1, Pallas kernels, per_device(): pl.pallas_call(functools.partial(kernel, n, kv_local, per_group, unroll),...  63 us
    unnamed x1, local copies, waits for them, and re-layouts  3.13 us

profile of v1, /device:TPU:31, one launch (start us, length us, event | category | flops | bytes accessed | tf_op | source)
XLA Modules:
  0.0 66.2 jit_solution(1597471411675854397)
XLA Ops:
  0.0 63.0 %shard_map.64 = bf16[256,4096]{1,0:T(8,128)(2,1)} custom-call(bf16[256,4096]{1,0:T(8,128)(2,1)} %q_ref.1, bf16[256,1024]{1,0:T(8,128)(2,1)} %k_ref.1, bf16[256,1024]{1,0:T(8,128)(2,1)} %v_ref.1, bf16[32,128,128]{2,1,0:T(8,128)(2,1)} %qmap_ref.1, bf16[8,128,128]{2,1,0:T(8,128)(2,1)} %kmap_ref.1, s32[1,256]{1,0:T(1,128)} %bitcast.1), custom_call_target="tpu_custom_call" | custom-call | tf_op jit(solution)/shard_map/pallas_call | solution.py:237
  63.0 3.1 %copy.8 = bf16[256,4096]{1,0:T(8,128)(2,1)} copy(bf16[256,4096]{1,0:T(8,128)(2,1)} %shard_map.64) | data formatting | bytes 4194304

commit v2 on v1

v2 whole, which is shorter than its diff:
```python
import functools
import math

import jax
import jax.numpy as jnp
from jax import lax
from jax.experimental import pallas as pl
from jax.experimental.pallas import tpu as pltpu
from jax.sharding import PartitionSpec as P

QHEADS = 128
KVH = 8
LENGTH = 131072
epsilon = 1e-06
masked_score = -1e30
MESH = pl.DeviceIdType.MESH
LOG2E = 1.4426950408889634
OWN_UNROLL = 8
UNROLL = 8
STEP_HEADS = 8


def elu_plus_one(x):
    return jnp.where(x > 0.0, x + 1.0, jnp.exp2(jnp.minimum(x, 0.0) * LOG2E))


def angle_parts(positions):
    angles = (0.5 * math.pi / LENGTH) * positions.astype(jnp.float32)
    return jnp.cos(angles), jnp.sin(angles)


def nt_dot(a, b):
    return lax.dot_general(a, b, (((1,), (1,)), ((), ())), preferred_element_type=jnp.float32)


def nn_dot(a, b):
    return jnp.dot(a, b, preferred_element_type=jnp.float32)


def causal_mask(size):
    row = lax.broadcasted_iota(jnp.int32, (size, size), 0)
    col = lax.broadcasted_iota(jnp.int32, (size, size), 1)
    return row >= col


def teacher_kernel(
    n, kv_local, per_group, own_unroll, unroll,
    q_hbm, k_hbm, v_hbm, kmap_ref, pos_ref,
    out_hbm, feats_ref, stacked_ref, cos_ref, sin_ref,
    q_ref, kbuf, vbuf, pbuf, acc, top, state, tbuf,
    local_sem, out_sem, send_sem, recv_sem, fwd_sem,
):
    tokens, hd = cos_ref.shape
    heads = kv_local * per_group
    nz = n // 2
    me = lax.axis_index("seq")
    z = me // 2
    core = me % 2
    partner = z * 2 + 1 - core
    group0 = lax.axis_index("head") * heads // (QHEADS // KVH)
    width = kv_local * hd
    columns = pl.ds(pl.multiple_of(group0 * hd, hd), width)
    scaling = LOG2E / math.sqrt(hd)

    local = (
        pltpu.make_async_copy(k_hbm.at[:, columns], kbuf.at[me], local_sem.at[0]),
        pltpu.make_async_copy(v_hbm.at[:, columns], vbuf.at[me], local_sem.at[1]),
        pltpu.make_async_copy(q_hbm, q_ref, local_sem.at[2]),
    )
    for copy in local:
        copy.start()

    barrier = pltpu.get_barrier_semaphore()

    def greet(zp, carry):
        pl.semaphore_signal(barrier, inc=1, device_id={"seq": zp * 2 + core}, device_id_type=MESH)
        return carry

    lax.fori_loop(0, z, greet, 0)
    lax.fori_loop(z + 1, nz, greet, 0)
    pl.semaphore_signal(barrier, inc=1, device_id={"seq": partner}, device_id_type=MESH)
    pl.semaphore_wait(barrier, nz)

    own = (k_hbm.at[:, columns], v_hbm.at[:, columns], pos_ref)
    buffers = (kbuf, vbuf, pbuf)

    def own_copy(part, slot, target):
        return pltpu.make_async_remote_copy(
            src_ref=own[part], dst_ref=buffers[part].at[me],
            send_sem=send_sem.at[part, slot], recv_sem=recv_sem.at[part, me],
            device_id={"seq": target}, device_id_type=MESH,
        )

    def forward_copy(part, zp):
        block = zp * 2 + core
        return pltpu.make_async_remote_copy(
            src_ref=buffers[part].at[block], dst_ref=buffers[part].at[block],
            send_sem=fwd_sem.at[part, zp], recv_sem=recv_sem.at[part, block],
            device_id={"seq": partner}, device_id_type=MESH,
        )

    def arrival(part, block):
        return pltpu.make_async_remote_copy(
            src_ref=buffers[part].at[block], dst_ref=buffers[part].at[block],
            send_sem=send_sem.at[part, 0], recv_sem=recv_sem.at[part, block],
            device_id={"seq": partner}, device_id_type=MESH,
        )

    @pl.when(core == 0)
    def _():
        for part in range(3):
            own_copy(part, z, partner).start()

    def send_up(zp, carry):
        for part in range(3):
            own_copy(part, zp, zp * 2 + core).start()
        return carry

    lax.fori_loop(z + 1, nz, send_up, 0)

    def take_and_forward(zp):
        @pl.when(zp >= 0)
        def _():
            for part in range(3):
                arrival(part, zp * 2 + core).wait_recv()
            for part in range(3):
                forward_copy(part, zp).start()

    def with_ones(values):
        return jnp.concatenate([values, jnp.ones(values.shape, jnp.bfloat16)], axis=1)

    def key_feats(keys, group, positions):
        cosine, sine = angle_parts(positions)
        projected = nn_dot(keys, kmap_ref[group0 + group]).T
        mapped = elu_plus_one(projected)
        return jnp.concatenate([cosine * mapped, sine * mapped], axis=0).astype(jnp.bfloat16)

    def query(h):
        return q_ref[:, pl.ds(pl.multiple_of(h * hd, hd), hd)]

    tall = jnp.broadcast_to(pos_ref[...].astype(jnp.float32), (hd, tokens)).T
    cosine, sine = angle_parts(tall)
    cos_ref[...] = cosine
    sin_ref[...] = sine
    for copy in local:
        copy.wait()

    tile = math.gcd(tokens, 128)
    for g in range(kv_local):
        group_cols = slice(g * hd, (g + 1) * hd)
        keys = kbuf[me, :, group_cols]
        values = with_ones(vbuf[me, :, group_cols])
        feats_ref[g] = key_feats(keys, g, pos_ref[...])
        state[g] = jnp.zeros((2 * hd, 2 * hd), jnp.float32)

        def own_body(i, carry, g=g, keys=keys, values=values):
            mask = causal_mask(tile)
            for u in range(own_unroll):
                h = g * per_group + i * own_unroll + u
                scores = nt_dot(query(h), keys)
                rows = []
                for t in range(0, tokens, tile):
                    pieces = [scores[t : t + tile, c : c + tile] * scaling for c in range(0, t + tile, tile)]
                    pieces[-1] = jnp.where(mask, pieces[-1], masked_score)
                    kept = jnp.concatenate(pieces, axis=1)
                    largest = jnp.max(kept, axis=1, keepdims=True)
                    part = jnp.exp2(kept - largest).astype(jnp.bfloat16)
                    if t + tile < tokens:
                        part = jnp.concatenate(
                            [part, jnp.zeros((tile, tokens - t - tile), jnp.bfloat16)], axis=1
                        )
                    rows.append(part)
                    top[h, t : t + tile, :] = jnp.broadcast_to(largest, (tile, hd))
                acc[h] = nn_dot(jnp.concatenate(rows, axis=0), values)
            return carry

        lax.fori_loop(0, per_group // own_unroll, own_body, 0)
        if g == 0:
            take_and_forward(z - 1)

    def use_blocks(first, count, per_step, following):
        span = count * tokens
        for g in range(kv_local):
            group_cols = slice(g * hd, (g + 1) * hd)
            keys = kbuf[pl.ds(first, count), :, group_cols].reshape(span, hd)
            values = with_ones(vbuf[pl.ds(first, count), :, group_cols].reshape(span, hd))
            positions = jnp.concatenate([pbuf[first + b] for b in range(count)], axis=1)
            state[g] += nn_dot(key_feats(keys, g, positions), values)

            def body(i, carry, g=g, keys=keys, values=values):
                for u in range(per_step):
                    h = g * per_group + i * per_step + u
                    scores = nt_dot(query(h), keys) * scaling
                    before = top[h]
                    largest = jnp.maximum(before, jnp.max(scores, axis=1, keepdims=True))
                    factor = jnp.exp2(before - largest)
                    wide = jnp.concatenate([largest] * (span // hd), axis=1)
                    weights = jnp.exp2(scores - wide).astype(jnp.bfloat16)
                    acc[h] = acc[h] * jnp.concatenate([factor, factor], axis=1) + nn_dot(weights, values)
                    top[h] = largest
                return carry

            lax.fori_loop(0, per_group // per_step, body, 0)
            if g == 0 and following is not None:
                take_and_forward(following)

    @pl.when(core == 1)
    def _():
        for part in range(3):
            arrival(part, partner).wait_recv()
        use_blocks(partner, 1, own_unroll, None)

    def step(i, carry):
        zp = z - 1 - i
        for part in range(3):
            arrival(part, zp * 2 + 1 - core).wait_recv()
        use_blocks(zp * 2, 2, unroll, zp - 1)
        return carry

    lax.fori_loop(0, z, step, 0)

    for g in range(kv_local):
        stacked_ref[g, :tokens, :] = with_ones(vbuf[me, :, g * hd : (g + 1) * hd])
        stacked_ref[g, tokens:, :] = state[g].astype(jnp.bfloat16)

        def last_body(i, carry, g=g):
            for u in range(own_unroll):
                h = g * per_group + i * own_unroll + u
                tbuf[:, pl.ds(pl.multiple_of(h * hd, hd), hd)] = (
                    acc[h, :, :hd] * reciprocal(acc[h, :, hd:])
                ).astype(jnp.bfloat16)
            return carry

        lax.fori_loop(0, per_group // own_unroll, last_body, 0)
        part_cols = pl.ds(g * per_group * hd, per_group * hd)
        pltpu.make_async_copy(tbuf.at[:, part_cols], out_hbm.at[:, part_cols], out_sem.at[g]).start()

    @pl.when(core == 0)
    def _():
        for part in range(3):
            own_copy(part, z, partner).wait_send()

    def sent(zp, carry):
        for part in range(3):
            own_copy(part, zp, zp * 2 + core).wait_send()
        return carry

    lax.fori_loop(z + 1, nz, sent, 0)

    def forwarded(zp, carry):
        for part in range(3):
            forward_copy(part, zp).wait_send()
        return carry

    lax.fori_loop(0, z, forwarded, 0)
    for g in range(kv_local):
        part_cols = pl.ds(g * per_group * hd, per_group * hd)
        pltpu.make_async_copy(tbuf.at[:, part_cols], out_hbm.at[:, part_cols], out_sem.at[g]).wait()


def reciprocal(x):
    guess = pl.reciprocal(x, approx=True)
    return guess * (2.0 - x * guess)


def student_kernel(step_heads, q_ref, qmap_ref, teacher_ref, feats_ref, stacked_ref, cos_ref, sin_ref, out_ref):
    tokens, hd = cos_ref.shape
    tile = math.gcd(tokens, 128)
    mask = causal_mask(tile)
    for u in range(step_heads):
        cols = slice(u * hd, (u + 1) * hd)
        mapped = elu_plus_one(nn_dot(q_ref[:, cols], qmap_ref[u]))
        qf = jnp.concatenate([cos_ref[...] * mapped, sin_ref[...] * mapped], axis=1).astype(jnp.bfloat16)
        inner = nn_dot(qf, feats_ref[0])
        rows = []
        for t in range(0, tokens, tile):
            pieces = [inner[t : t + tile, c : c + tile] for c in range(0, t + tile, tile)]
            pieces[-1] = jnp.where(mask, pieces[-1], 0.0)
            if t + tile < tokens:
                pieces.append(jnp.zeros((tile, tokens - t - tile), jnp.float32))
            rows.append(jnp.concatenate(pieces, axis=1).astype(jnp.bfloat16))
        both = nn_dot(jnp.concatenate([jnp.concatenate(rows, axis=0), qf], axis=1), stacked_ref[0])
        student = both[:, :hd] * reciprocal(both[:, hd:] + epsilon)
        out_ref[:, cols] = (2.0 * (student - teacher_ref[:, cols].astype(jnp.float32))).astype(jnp.bfloat16)


def per_device(n, queries, keys, values, query_map, key_map, positions):
    tokens = queries.shape[0]
    hd = key_map.shape[1]
    heads = query_map.shape[0]
    kv_local = max(1, heads // (QHEADS // KVH))
    per_group = heads // kv_local
    own_unroll = math.gcd(per_group, OWN_UNROLL)
    unroll = math.gcd(per_group, UNROLL)
    width = kv_local * hd
    vmem = pl.BlockSpec(memory_space=pltpu.VMEM)
    hbm = pl.BlockSpec(memory_space=pl.ANY)
    teacher, feats, stacked, cosine, sine = pl.pallas_call(
        functools.partial(teacher_kernel, n, kv_local, per_group, own_unroll, unroll),
        out_shape=(
            jax.ShapeDtypeStruct(queries.shape, jnp.bfloat16),
            jax.ShapeDtypeStruct((kv_local, 2 * hd, tokens), jnp.bfloat16),
            jax.ShapeDtypeStruct((kv_local, tokens + 2 * hd, 2 * hd), jnp.bfloat16),
            jax.ShapeDtypeStruct((tokens, hd), jnp.float32),
            jax.ShapeDtypeStruct((tokens, hd), jnp.float32),
        ),
        in_specs=[hbm, hbm, hbm, vmem, vmem],
        out_specs=[hbm, vmem, vmem, vmem, vmem],
        scratch_shapes=[
            pltpu.VMEM((tokens, heads * hd), jnp.bfloat16),
            pltpu.VMEM((n, tokens, width), jnp.bfloat16),
            pltpu.VMEM((n, tokens, width), jnp.bfloat16),
            pltpu.VMEM((n, 1, tokens), jnp.int32),
            pltpu.VMEM((heads, tokens, 2 * hd), jnp.float32),
            pltpu.VMEM((heads, tokens, hd), jnp.float32),
            pltpu.VMEM((kv_local, 2 * hd, 2 * hd), jnp.float32),
            pltpu.VMEM((tokens, heads * hd), jnp.bfloat16),
            pltpu.SemaphoreType.DMA((3,)),
            pltpu.SemaphoreType.DMA((kv_local,)),
            pltpu.SemaphoreType.DMA((3, n)),
            pltpu.SemaphoreType.DMA((3, n)),
            pltpu.SemaphoreType.DMA((3, n)),
        ],
        compiler_params=pltpu.CompilerParams(
            collective_id=0, has_side_effects=True, vmem_limit_bytes=56 * 1024 * 1024
        ),
    )(queries, keys, values, key_map, positions.reshape(1, tokens))

    step_heads = math.gcd(per_group, STEP_HEADS)
    by_columns = pl.BlockSpec((tokens, step_heads * hd), lambda i: (0, i))
    by_group = lambda rows, cols: pl.BlockSpec((1, rows, cols), lambda i: (i * step_heads // per_group, 0, 0))
    whole = pl.BlockSpec((tokens, hd), lambda i: (0, 0))
    return pl.pallas_call(
        functools.partial(student_kernel, step_heads),
        grid=(heads // step_heads,),
        out_shape=jax.ShapeDtypeStruct(queries.shape, jnp.bfloat16),
        in_specs=[
            by_columns,
            pl.BlockSpec((step_heads, hd, hd), lambda i: (i, 0, 0)),
            by_columns,
            by_group(2 * hd, tokens),
            by_group(tokens + 2 * hd, 2 * hd),
            whole,
            whole,
        ],
        out_specs=by_columns,
        compiler_params=pltpu.CompilerParams(vmem_limit_bytes=48 * 1024 * 1024),
    )(queries, query_map, teacher, feats, stacked, cosine, sine)


def solution(mesh):
    in_specs = (
        P("seq", "head"),
        P("seq", None),
        P("seq", None),
        P("head", None, None),
        P(),
        P("seq"),
    )
    return jax.shard_map(
        functools.partial(per_device, mesh.shape["seq"]),
        mesh=mesh, in_specs=in_specs, out_specs=P("seq", "head"), check_vma=False,
    )
```

time: 66.3 us -> 66.1 us (level); the launches traced: 66.2 us -> 64.9 us
  Pallas kernels: 63 us -> 61.1 us
  local copies, waits for them, and re-layouts: 3.13 us -> 3.8 us
    pallas_call x1 -> x2, Pallas kernels: 63 us -> 61.1 us  [the longest x1 51.8 us: per_device(): pl.pallas_call(functools.partial(teacher_kernel, n, kv_local, per_group,...]
    unnamed x1 -> x12, local copies, waits for them, and re-layouts: 3.13 us -> 3.8 us
where the time goes in v2:
time: 66.1 us; the launch traced here: 64.9 us
  Pallas kernels  61.1 us (92%)
  local copies, waits for them, and re-layouts  3.8 us (6%)
    pallas_call x1, Pallas kernels, per_device(): pl.pallas_call(functools.partial(teacher_kernel, n, kv_local, per_group,...  51.8 us
    pallas_call x1, Pallas kernels, per_device(): pl.pallas_call(functools.partial(student_kernel, step_heads), grid=(heads...  9.34 us
    unnamed x12, local copies, waits for them, and re-layouts  3.8 us

profile of v2, /device:TPU:31, one launch (start us, length us, event | category | flops | bytes accessed | tf_op | source)
XLA Modules:
  0.0 64.9 jit_solution(358053735937351260)
XLA Ops:
  0.0 0.0 copy-start
  0.0 0.0 copy-start.1
  0.0 51.8 %shard_map.64 = (bf16[256,4096]{1,0:T(8,128)(2,1)}, bf16[2,256,256]{2,1,0:T(8,128)(2,1)}, bf16[2,512,256]{2,1,0:T(8,128)(2,1)}, f32[256,128]{1,0:T(8,128)}, f32[256,128]{1,0:T(8,128)}) custom-call(bf16[256,4096]{1,0:T(8,128)(2,1)} %q_ref.1, bf16[256,1024]{1,0:T(8,128)(2,1)} %k_hbm.1, bf16[256,1024]{1,0:T(8,128)(2,1)} %v_hbm.1, ...), custom_call_target="tpu_custom_call" | custom-call | tf_op jit(solution)/shard_map/pallas_call | solution.py:298
  51.8 0.0 copy-done
  51.8 0.0 copy-done.1
  51.8 0.0 copy-start.2
  51.8 1.0 %copy-done.2 = bf16[2,512,256]{2,1,0:T(8,128)(2,1)S(1)} copy-done((bf16[2,512,256]{2,1,0:T(8,128)(2,1)S(1)}, bf16[2,512,256]{2,1,0:T(8,128)(2,1)}, u32[]{:S(2)}) %copy-start.2) | copy-done | bytes 524312
  52.8 0.0 copy-start.3
  52.8 0.9 %copy-done.3 = bf16[2,256,256]{2,1,0:T(8,128)(2,1)S(1)} copy-done((bf16[2,256,256]{2,1,0:T(8,128)(2,1)S(1)}, bf16[2,256,256]{2,1,0:T(8,128)(2,1)}, u32[]{:S(2)}) %copy-start.3) | copy-done | bytes 262168
  53.8 0.0 copy-start.4
  53.8 0.9 %copy-done.4 = f32[256,128]{1,0:T(8,128)S(1)} copy-done((f32[256,128]{1,0:T(8,128)S(1)}, f32[256,128]{1,0:T(8,128)}, u32[]{:S(2)}) %copy-start.4) | copy-done | bytes 131096
  54.7 0.0 copy-start.5
  54.7 0.9 %copy-done.5 = f32[256,128]{1,0:T(8,128)S(1)} copy-done((f32[256,128]{1,0:T(8,128)S(1)}, f32[256,128]{1,0:T(8,128)}, u32[]{:S(2)}) %copy-start.5) | copy-done | bytes 131096
  55.6 9.3 %shard_map.65 = bf16[256,4096]{1,0:T(8,128)(2,1)} custom-call(bf16[256,4096]{1,0:T(8,128)(2,1)S(1)} %copy-done, bf16[32,128,128]{2,1,0:T(8,128)(2,1)S(1)} %copy-done.1, bf16[256,4096]{1,0:T(8,128)(2,1)} %get-tuple-element.10.teacher_ref, bf16[2,256,256]{2,1,0:T(8,128)(2,1)S(1)} %copy-done.3, bf16[2,512,256]{2,1,0:T(8,128)(2,1)S(1)} %copy-done.2, ...), custom_call_target="tpu_custom_call" | custom-call | tf_op jit(solution)/shard_map/pallas_call | solution.py:333
Async XLA Ops:
  0.0 51.8 %copy-start = (bf16[256,4096]{1,0:T(8,128)(2,1)S(1)}, bf16[256,4096]{1,0:T(8,128)(2,1)}, u32[]{:S(2)}) copy-start(bf16[256,4096]{1,0:T(8,128)(2,1)} %q_ref.1) | copy-start | bytes 6291460
  0.0 51.8 %copy-start.1 = (bf16[32,128,128]{2,1,0:T(8,128)(2,1)S(1)}, bf16[32,128,128]{2,1,0:T(8,128)(2,1)}, u32[]{:S(2)}) copy-start(bf16[32,128,128]{2,1,0:T(8,128)(2,1)} %qmap_ref.1) | copy-start | bytes 3145732
  51.8 1.0 %copy-start.2 = (bf16[2,512,256]{2,1,0:T(8,128)(2,1)S(1)}, bf16[2,512,256]{2,1,0:T(8,128)(2,1)}, u32[]{:S(2)}) copy-start(bf16[2,512,256]{2,1,0:T(8,128)(2,1)} %get-tuple-element.12.stacked_ref) | copy-start | bytes 1572868
  52.8 0.9 %copy-start.3 = (bf16[2,256,256]{2,1,0:T(8,128)(2,1)S(1)}, bf16[2,256,256]{2,1,0:T(8,128)(2,1)}, u32[]{:S(2)}) copy-start(bf16[2,256,256]{2,1,0:T(8,128)(2,1)} %get-tuple-element.11.feats_ref) | copy-start | bytes 786436
  53.8 0.9 %copy-start.4 = (f32[256,128]{1,0:T(8,128)S(1)}, f32[256,128]{1,0:T(8,128)}, u32[]{:S(2)}) copy-start(f32[256,128]{1,0:T(8,128)} %get-tuple-element.13.cos_ref) | copy-start | bytes 393220
  54.7 0.9 %copy-start.5 = (f32[256,128]{1,0:T(8,128)S(1)}, f32[256,128]{1,0:T(8,128)}, u32[]{:S(2)}) copy-start(f32[256,128]{1,0:T(8,128)} %get-tuple-element.14.sin_ref) | copy-start | bytes 393220

commit v3 on v2

--- a/solution.py
+++ b/solution.py
@@ -15,9 +15,9 @@
 masked_score = -1e30
 MESH = pl.DeviceIdType.MESH
 LOG2E = 1.4426950408889634
-OWN_UNROLL = 8
-UNROLL = 8
-STEP_HEADS = 8
+OWN_UNROLL = 16
+UNROLL = 16
+STEP_HEADS = 16
 
 
 def elu_plus_one(x):
@@ -322,7 +322,7 @@
             pltpu.SemaphoreType.DMA((3, n)),
         ],
         compiler_params=pltpu.CompilerParams(
-            collective_id=0, has_side_effects=True, vmem_limit_bytes=56 * 1024 * 1024
+            collective_id=0, has_side_effects=True, vmem_limit_bytes=61 * 1024 * 1024
         ),
     )(queries, keys, values, key_map, positions.reshape(1, tokens))
 
@@ -344,7 +344,7 @@
             whole,
         ],
         out_specs=by_columns,
-        compiler_params=pltpu.CompilerParams(vmem_limit_bytes=48 * 1024 * 1024),
+        compiler_params=pltpu.CompilerParams(vmem_limit_bytes=61 * 1024 * 1024),
     )(queries, query_map, teacher, feats, stacked, cosine, sine)
 
 

time: 66.1 us -> 58 us (0.88)
  Pallas kernels: 61.1 us -> 56.9 us
  local copies, waits for them, and re-layouts: 3.8 us -> 0 us
    pallas_call x1, Pallas kernels: 51.8 us -> 46.7 us  [per_device(): pl.pallas_call(functools.partial(teacher_kernel, n, kv_local, per_group,...]
    unnamed x12 -> x0, local copies, waits for them, and re-layouts: 3.8 us -> none
    pallas_call x1, Pallas kernels: 9.34 us -> 10.2 us  [per_device(): pl.pallas_call(functools.partial(student_kernel, step_heads), grid=(heads...]
where the time goes in v3:
time: 58 us; the launch traced here: 56.9 us
  Pallas kernels  56.9 us (98%)
    pallas_call x1, Pallas kernels, per_device(): pl.pallas_call(functools.partial(teacher_kernel, n, kv_local, per_group,...  46.7 us
    pallas_call x1, Pallas kernels, per_device(): pl.pallas_call(functools.partial(student_kernel, step_heads), grid=(heads...  10.2 us

profile of v3, /device:TPU:31, one launch (start us, length us, event | category | flops | bytes accessed | tf_op | source)
XLA Modules:
  0.0 56.9 jit_solution(12797168132725281841)
XLA Ops:
  0.0 46.7 %shard_map.64 = (bf16[256,4096]{1,0:T(8,128)(2,1)}, bf16[2,256,256]{2,1,0:T(8,128)(2,1)}, bf16[2,512,256]{2,1,0:T(8,128)(2,1)}, f32[256,128]{1,0:T(8,128)}, f32[256,128]{1,0:T(8,128)}) custom-call(bf16[256,4096]{1,0:T(8,128)(2,1)} %q_ref.1, bf16[256,1024]{1,0:T(8,128)(2,1)} %k_hbm.1, bf16[256,1024]{1,0:T(8,128)(2,1)} %v_hbm.1, ...), custom_call_target="tpu_custom_call" | custom-call | tf_op jit(solution)/shard_map/pallas_call | solution.py:298
  46.7 10.2 %shard_map.65 = bf16[256,4096]{1,0:T(8,128)(2,1)} custom-call(bf16[256,4096]{1,0:T(8,128)(2,1)} %q_ref.1, bf16[32,128,128]{2,1,0:T(8,128)(2,1)} %qmap_ref.1, bf16[256,4096]{1,0:T(8,128)(2,1)} %get-tuple-element.10.teacher_ref, bf16[2,256,256]{2,1,0:T(8,128)(2,1)} %get-tuple-element.11.feats_ref, bf16[2,512,256]{2,1,0:T(8,128)(2,1)} %get-tuple-element.12.stacked_ref, ...), custom_call_target="tpu_custom_call" | custom-call | tf_op jit(solution)/shard_map/pallas_call | solution.py:333
